TPU v7x, 32 devices: a whole 2x2x4 slice. The times are simulated.
32 devices in a mesh: chain: 4 (over z), tech: 4 (over x, core), blk: 2 (over y).
Axes of the slice: x: 2, y: 2, z: 4, core: 2. Of those that a mesh axis runs over, the one named last changes fastest.
Arguments:
- block_inverse: bfloat16 [4, 4, 3072, 3072], P('tech', 'chain', 'blk'), may hold values from -1 to 4.5, as said below
- coupling: bfloat16 [4, 4, 3072, 512], P('tech', 'chain', 'blk'), may hold values from -0.0390625 to 0.0390625
- data_rhs: bfloat16 [4, 4, 3072, 256], P('tech', 'chain', 'blk'), may hold values from -6 to 6
- station_seen: int32 [4, 4, 1024], P('tech', 'chain', 'blk'), may hold values 0 or 1
- shared_inverse: float32 [4, 512, 512], P('chain'), may hold values from -0.05 to 1, as said below
- walk_weight: float32 [512], replicated, may hold values from 0.92 to 1
- shared_rhs: float32 [4, 512, 256], P('chain'), may hold values from -1.2 to 1.2
Outputs:
- coords: float32 [4, 4, 3072, 256], P('tech', 'chain', 'blk')
- shared: float32 [4, 512, 256], P('chain')
Inputs may be any that keep to these rules, and one draw needn't show every extreme that they name: `block_inverse`: each block is symmetric. `shared_inverse`: each block is symmetric.
All inputs are finite; a program needn't handle non-finite values. No bound on the sum of `station_seen` on one device may be relied on, other than what follows from the above.
Results may differ from a plain program's by a relative error of at most 0.004.
Values may be sent and summed in bfloat16 or wider, within the bound.
A program may use at most 128 MiB of HBM per device.

v0:
```python
import jax
import jax.numpy as jnp
from jax import lax
from jax.sharding import PartitionSpec as P

SWEEPS = 2


def shifted(block, axis, distance):
    devices = range(lax.axis_size(axis))
    route = [(i - distance, i) for i in devices if i - distance in devices]
    return lax.ppermute(block, axis, route)


def add_columns(matrix, piece):
    return jnp.dot(matrix, piece, preferred_element_type=jnp.float32)


def shards(
    block_inverse, coupling, data_rhs, station_seen, shared_inverse, walk_weight, shared_rhs
):
    inverse_rows = block_inverse[0, 0]
    coupling_rows = coupling[0, 0]
    rhs_rows = data_rhs[0, 0].astype(jnp.float32)
    station_count = station_seen.shape[2]
    seen_rows = (
        jnp.broadcast_to(station_seen[0, 0][:, None], (station_count, 3))
        .reshape(-1)
        .astype(jnp.float32)
    )
    week_inverse = shared_inverse[0]
    step_matrix = week_inverse * walk_weight[None, :]
    week_rhs = shared_rhs[0]
    position = lax.axis_index("chain")
    length = lax.axis_size("chain")
    half_rows = inverse_rows.shape[0]
    columns_count = rhs_rows.shape[1]
    shared = jnp.zeros_like(week_rhs)
    coords = jnp.zeros((half_rows, columns_count), jnp.float32)
    for sweep_index in range(SWEEPS):
        if sweep_index > 0:
            later = shifted(shared, "chain", -1)
        else:
            later = jnp.zeros_like(shared)
        product = jnp.dot(
            coupling_rows, shared.astype(jnp.bfloat16), preferred_element_type=jnp.float32
        )
        residual_low = (rhs_rows - product).astype(jnp.bfloat16)
        solved = add_columns(inverse_rows, lax.all_gather(residual_low, "blk", axis=0, tiled=True))
        coords = seen_rows[:, None] * solved
        partial_terms = lax.dot_general(
            coupling_rows,
            coords.astype(jnp.bfloat16),
            (((0,), (0,)), ((), ())),
            preferred_element_type=jnp.float32,
        )
        station_sum = lax.psum(partial_terms, ("tech", "blk"))
        offset = jnp.dot(
            week_inverse,
            week_rhs + walk_weight[:, None] * later - station_sum,
            precision=lax.Precision.HIGHEST,
        )

        def relay(turn, current):
            incoming = shifted(current, "chain", 1)
            update = offset + jnp.dot(step_matrix, incoming, precision=lax.Precision.HIGHEST)
            return jnp.where(position == turn, update, current)

        shared = lax.fori_loop(0, length, relay, jnp.zeros_like(offset))
    return (coords[None, None], shared[None])


def solution(mesh):
    in_specs = (
        P("tech", "chain", "blk", None),
        P("tech", "chain", "blk", None),
        P("tech", "chain", "blk", None),
        P("tech", "chain", "blk"),
        P("chain", None, None),
        P(),
        P("chain", None, None),
    )
    out_specs = (P("tech", "chain", "blk", None), P("chain", None, None))
    return jax.shard_map(shards, mesh=mesh, in_specs=in_specs, out_specs=out_specs, check_vma=False)
```

profile of v0, /device:TPU:25, one launch (start us, length us, event | category | flops | bytes accessed | tf_op | source)
XLA Modules:
  0.0 344.0 jit_solution(165662870213947665)
XLA Ops:
  11.6 27.9 %all-gather.3.cloned.1.call-done = bf16[3072,256]{1,0:T(8,128)(2,1)} async-done(((bf16[1536,256]{1,0:T(8,128)(2,1)}), bf16[3072,256]{1,0:T(8,128)(2,1)}) %all-gather.3.cloned.1.call-update) | async-done | bytes 1572880 | tf_op jit(solution)/shard_map/all_gather | solution.py:49
  39.5 8.2 %fusion.25 = f32[512,256]{1,0:T(8,128)} fusion(bf16[1,1,1536,512]{3,2,1,0:T(8,128)(2,1)S(1)} %copy-done, bf16[3072,256]{1,0:T(8,128)(2,1)} %all-gather.3.cloned.1.call-done, bf16[1,1,1536,3072]{3,2,1,0:T(8,128)(2,1)} %param.11, f32[1536]{0:T(1024)S(1)} %convert_element_type.40), kind=kOutput, calls=%fused_computation.26 | convolution fusion | flops 2819358720 | bytes 13113344 | tf_op jit(solution)/shard_map/dot_general | solution.py:51
  49.2 52.3 %all-reduce.3.cloned.1.call-done = f32[512,256]{1,0:T(8,128)} async-done(((f32[512,256]{1,0:T(8,128)}), f32[512,256]{1,0:T(8,128)}) %all-reduce.3.cloned.1.call-update) | async-done | bytes 524304 | tf_op jit(solution)/shard_map/psum | solution.py:57
  101.5 3.5 %convolution_bitcast_fusion.3 = f32[512,256]{0,1:T(8,128)S(1)} fusion(f32[1,512,512]{2,1,0:T(8,128)} %param.15, f32[512,256]{1,0:T(8,128)} %all-reduce.3.cloned.1.call-done, f32[1,512,256]{2,1,0:T(8,128)} %param.17, f32[512]{0:T(512)S(1)} %broadcast_multiply_fusion), kind=kOutput, calls=%fused_computation.29 | convolution fusion | flops 805568512 | bytes 2623488 | tf_op jit(solution)/shard_map/dot_general | solution.py:58
  106.0 65.0 %while.28 = (s32[]{:T(128)}, f32[512,256]{1,0:T(8,128)}, s32[]{:T(128)}, f32[512,512]{1,0:T(8,128)S(1)}, f32[512,256]{1,0:T(8,128)}, /*index=5*/s32[]{:T(128)}, s32[]{:T(128)}) while((s32[]{:T(128)}, f32[512,256]{1,0:T(8,128)}, s32[]{:T(128)}, f32[512,512]{1,0:T(8,128)S(1)}, f32[512,256]{1,0:T(8,128)}, /*index=5*/s32[]{:T(128)}, ...), condition=%wide.region_2.3_spmd.clone, body=%wide.region_1.2_spmd.clone.sunk | while | flops 805699584 | bytes 6291593 | solution.py:69
  107.4 12.5 %collective-permute-done = f32[512,256]{1,0:T(8,128)} collective-permute-done((f32[512,256]{1,0:T(8,128)S(1)}, f32[512,256]{1,0:T(8,128)}, u32[]{:S(2)}, u32[]{:S(2)}) %collective-permute-start) | collective-permute-done | bytes 524320 | tf_op jit(solution)/shard_map/while/body/eval_jaxpr/ppermute | solution.py:12
  119.9 3.0 fusion.65
  125.3 11.6 %collective-permute-done = f32[512,256]{1,0:T(8,128)} collective-permute-done((f32[512,256]{1,0:T(8,128)S(1)}, f32[512,256]{1,0:T(8,128)}, u32[]{:S(2)}, u32[]{:S(2)}) %collective-permute-start) | collective-permute-done | bytes 524320 | tf_op jit(solution)/shard_map/while/body/eval_jaxpr/ppermute | solution.py:12
  136.9 3.0 fusion.65
  142.2 10.7 %collective-permute-done = f32[512,256]{1,0:T(8,128)} collective-permute-done((f32[512,256]{1,0:T(8,128)S(1)}, f32[512,256]{1,0:T(8,128)}, u32[]{:S(2)}, u32[]{:S(2)}) %collective-permute-start) | collective-permute-done | bytes 524320 | tf_op jit(solution)/shard_map/while/body/eval_jaxpr/ppermute | solution.py:12
  152.9 3.0 fusion.65
  158.3 9.8 %collective-permute-done = f32[512,256]{1,0:T(8,128)} collective-permute-done((f32[512,256]{1,0:T(8,128)S(1)}, f32[512,256]{1,0:T(8,128)}, u32[]{:S(2)}, u32[]{:S(2)}) %collective-permute-start) | collective-permute-done | bytes 524320 | tf_op jit(solution)/shard_map/while/body/eval_jaxpr/ppermute | solution.py:12
  168.0 3.0 fusion.65
  176.9 28.6 %all-gather.5.cloned.1.call-done = bf16[3072,256]{1,0:T(8,128)(2,1)} async-done(((bf16[1536,256]{1,0:T(8,128)(2,1)}), bf16[3072,256]{1,0:T(8,128)(2,1)}) %all-gather.5.cloned.1.call-update) | async-done | bytes 1572880 | tf_op jit(solution)/shard_map/all_gather | solution.py:49
  205.5 5.8 %fusion.9 = f32[256,1536]{1,0:T(8,128)S(1)} fusion(bf16[3072,256]{1,0:T(8,128)(2,1)} %all-gather.5.cloned.1.call-done, bf16[1,1,1536,3072]{3,2,1,0:T(8,128)(2,1)} %param.11, f32[1536]{0:T(1024)S(1)} %convert_element_type.40), kind=kOutput, calls=%fused_computation.11 | convolution fusion | flops 2416312320 | bytes 12589056 | tf_op jit(solution)/shard_map/dot_general | solution.py:16
  214.0 3.0 copy.14
  217.1 50.7 %all-reduce.5.cloned.1.call-done = f32[512,256]{1,0:T(8,128)} async-done(((f32[512,256]{1,0:T(8,128)}), f32[512,256]{1,0:T(8,128)}) %all-reduce.5.cloned.1.call-update) | async-done | bytes 524304 | tf_op jit(solution)/shard_map/psum | solution.py:57
  267.8 3.7 %convolution_bitcast_fusion.2 = f32[512,256]{0,1:T(8,128)S(1)} fusion(f32[1,512,512]{2,1,0:T(8,128)} %param.15, f32[512,256]{1,0:T(8,128)} %all-reduce.5.cloned.1.call-done, f32[1,512,256]{2,1,0:T(8,128)} %param.17, f32[512,256]{1,0:T(8,128)} %collective-permute-done.2, f32[512]{0:T(512)S(1)} %copy-done.3), kind=kOutput, calls=%fused_computation.28 | convolution fusion | flops 805699584 | bytes 3147776 | tf_op jit(solution)/shard_map/dot_general | solution.py:58
  272.5 65.0 %while.29 = (s32[]{:T(128)}, f32[512,256]{1,0:T(8,128)}, s32[]{:T(128)}, f32[512,512]{1,0:T(8,128)S(1)}, f32[512,256]{1,0:T(8,128)}, /*index=5*/s32[]{:T(128)}, s32[]{:T(128)}) while((s32[]{:T(128)}, f32[512,256]{1,0:T(8,128)}, s32[]{:T(128)}, f32[512,512]{1,0:T(8,128)S(1)}, f32[512,256]{1,0:T(8,128)}, /*index=5*/s32[]{:T(128)}, ...), condition=%wide.region_5.6_spmd.clone, body=%wide.region_4.5_spmd.clone.sunk | while | flops 805699584 | bytes 6291593 | solution.py:69
  273.8 12.5 %collective-permute-done.1 = f32[512,256]{1,0:T(8,128)} collective-permute-done((f32[512,256]{1,0:T(8,128)S(1)}, f32[512,256]{1,0:T(8,128)}, u32[]{:S(2)}, u32[]{:S(2)}) %collective-permute-start.1) | collective-permute-done | bytes 524320 | tf_op jit(solution)/shard_map/while/body/eval_jaxpr/ppermute | solution.py:12
  291.7 11.6 %collective-permute-done.1 = f32[512,256]{1,0:T(8,128)} collective-permute-done((f32[512,256]{1,0:T(8,128)S(1)}, f32[512,256]{1,0:T(8,128)}, u32[]{:S(2)}, u32[]{:S(2)}) %collective-permute-start.1) | collective-permute-done | bytes 524320 | tf_op jit(solution)/shard_map/while/body/eval_jaxpr/ppermute | solution.py:12
  308.7 10.7 %collective-permute-done.1 = f32[512,256]{1,0:T(8,128)} collective-permute-done((f32[512,256]{1,0:T(8,128)S(1)}, f32[512,256]{1,0:T(8,128)}, u32[]{:S(2)}, u32[]{:S(2)}) %collective-permute-start.1) | collective-permute-done | bytes 524320 | tf_op jit(solution)/shard_map/while/body/eval_jaxpr/ppermute | solution.py:12
  319.4 3.0 fusion.68
  324.7 9.8 %collective-permute-done.1 = f32[512,256]{1,0:T(8,128)} collective-permute-done((f32[512,256]{1,0:T(8,128)S(1)}, f32[512,256]{1,0:T(8,128)}, u32[]{:S(2)}, u32[]{:S(2)}) %collective-permute-start.1) | collective-permute-done | bytes 524320 | tf_op jit(solution)/shard_map/while/body/eval_jaxpr/ppermute | solution.py:12
  (51 shorter events, 42.2 us)
Async XLA Ops:
  7.2 1.4 copy-start
  7.2 4.0 %copy-start.4 = (s32[1,1,512]{2,1,0:T(1,128)S(1)}, s32[1,1,512]{2,1,0:T(1,128)}, u32[]{:S(2)}) copy-start(s32[1,1,512]{2,1,0:T(1,128)} %param.14) | copy-start | bytes 6148
  7.2 4.4 %copy-start.3 = (f32[512]{0:T(512)S(1)}, f32[512]{0:T(512)}, u32[]{:S(2)}) copy-start(f32[512]{0:T(512)} %param.16) | copy-start | bytes 6148
  7.2 32.3 %all-gather.3.cloned.1.call-start = ((), (), s32[]{:S(2)}) async-start(), calls=%async_computation | async-start | bytes 2359296 | tf_op jit(solution)/shard_map/all_gather | solution.py:49
  11.2 90.3 %all-reduce.3.cloned.1.call-start = ((), (), s32[]{:S(2)}) async-start(), calls=%async_computation.1 | async-start | bytes 1048576 | tf_op jit(solution)/shard_map/psum | solution.py:57
  47.8 157.7 %all-gather.5.cloned.1.call-start = ((), (), s32[]{:S(2)}) async-start(), calls=%async_computation.2 | async-start | bytes 2359296 | tf_op jit(solution)/shard_map/all_gather | solution.py:49
  106.1 13.8 %collective-permute-start = (f32[512,256]{1,0:T(8,128)S(1)}, f32[512,256]{1,0:T(8,128)}, u32[]{:S(2)}, u32[]{:S(2)}) collective-permute-start(f32[512,256]{1,0:T(8,128)S(1)} %broadcast_select_fusion.4), channel_id=1, source_target_pairs={{0,8},{8,16},{16,24},{1,9},{9,17},{17,25},{2,10},{10,18},{18,26},{... | collective-permute-start | bytes 1572872 | tf_op jit(solution)/shard_map/while/body/eval_jaxpr/ppermute | solution.py:12
  123.9 12.9 %collective-permute-start = (f32[512,256]{1,0:T(8,128)S(1)}, f32[512,256]{1,0:T(8,128)}, u32[]{:S(2)}, u32[]{:S(2)}) collective-permute-start(f32[512,256]{1,0:T(8,128)S(1)} %broadcast_select_fusion.4), channel_id=1, source_target_pairs={{0,8},{8,16},{16,24},{1,9},{9,17},{17,25},{2,10},{10,18},{18,26},{... | collective-permute-start | bytes 1572872 | tf_op jit(solution)/shard_map/while/body/eval_jaxpr/ppermute | solution.py:12
  140.9 12.0 %collective-permute-start = (f32[512,256]{1,0:T(8,128)S(1)}, f32[512,256]{1,0:T(8,128)}, u32[]{:S(2)}, u32[]{:S(2)}) collective-permute-start(f32[512,256]{1,0:T(8,128)S(1)} %broadcast_select_fusion.4), channel_id=1, source_target_pairs={{0,8},{8,16},{16,24},{1,9},{9,17},{17,25},{2,10},{10,18},{18,26},{... | collective-permute-start | bytes 1572872 | tf_op jit(solution)/shard_map/while/body/eval_jaxpr/ppermute | solution.py:12
  157.0 11.1 %collective-permute-start = (f32[512,256]{1,0:T(8,128)S(1)}, f32[512,256]{1,0:T(8,128)}, u32[]{:S(2)}, u32[]{:S(2)}) collective-permute-start(f32[512,256]{1,0:T(8,128)S(1)} %broadcast_select_fusion.4), channel_id=1, source_target_pairs={{0,8},{8,16},{16,24},{1,9},{9,17},{17,25},{2,10},{10,18},{18,26},{... | collective-permute-start | bytes 1572872 | tf_op jit(solution)/shard_map/while/body/eval_jaxpr/ppermute | solution.py:12
  171.0 2.9 copy-start.1
  173.9 93.9 %all-reduce.5.cloned.1.call-start = ((), (), s32[]{:S(2)}) async-start(), calls=%async_computation.3 | async-start | bytes 1048576 | tf_op jit(solution)/shard_map/psum | solution.py:57
  173.9 43.2 %collective-permute-start.2 = (f32[512,256]{1,0:T(8,128)S(1)}, f32[512,256]{1,0:T(8,128)}, u32[]{:S(2)}, u32[]{:S(2)}) collective-permute-start(f32[512,256]{1,0:T(8,128)S(1)} %copy-done.1), channel_id=1, source_target_pairs={{8,0},{16,8},{24,16},{9,1},{17,9},{25,17},{10,2},{18,10},{26,18},{... | collective-permute-start | bytes 1572872 | tf_op jit(solution)/shard_map/ppermute | solution.py:12
  211.3 1.2 copy-start.2
  272.5 13.8 %collective-permute-start.1 = (f32[512,256]{1,0:T(8,128)S(1)}, f32[512,256]{1,0:T(8,128)}, u32[]{:S(2)}, u32[]{:S(2)}) collective-permute-start(f32[512,256]{1,0:T(8,128)S(1)} %broadcast_select_fusion.5), channel_id=1, source_target_pairs={{0,8},{8,16},{16,24},{1,9},{9,17},{17,25},{2,10},{10,18},{18,26},{... | collective-permute-start | bytes 1572872 | tf_op jit(solution)/shard_map/while/body/eval_jaxpr/ppermute | solution.py:12
  290.4 12.9 %collective-permute-start.1 = (f32[512,256]{1,0:T(8,128)S(1)}, f32[512,256]{1,0:T(8,128)}, u32[]{:S(2)}, u32[]{:S(2)}) collective-permute-start(f32[512,256]{1,0:T(8,128)S(1)} %broadcast_select_fusion.5), channel_id=1, source_target_pairs={{0,8},{8,16},{16,24},{1,9},{9,17},{17,25},{2,10},{10,18},{18,26},{... | collective-permute-start | bytes 1572872 | tf_op jit(solution)/shard_map/while/body/eval_jaxpr/ppermute | solution.py:12
  307.4 12.0 %collective-permute-start.1 = (f32[512,256]{1,0:T(8,128)S(1)}, f32[512,256]{1,0:T(8,128)}, u32[]{:S(2)}, u32[]{:S(2)}) collective-permute-start(f32[512,256]{1,0:T(8,128)S(1)} %broadcast_select_fusion.5), channel_id=1, source_target_pairs={{0,8},{8,16},{16,24},{1,9},{9,17},{17,25},{2,10},{10,18},{18,26},{... | collective-permute-start | bytes 1572872 | tf_op jit(solution)/shard_map/while/body/eval_jaxpr/ppermute | solution.py:12
  323.4 11.1 %collective-permute-start.1 = (f32[512,256]{1,0:T(8,128)S(1)}, f32[512,256]{1,0:T(8,128)}, u32[]{:S(2)}, u32[]{:S(2)}) collective-permute-start(f32[512,256]{1,0:T(8,128)S(1)} %broadcast_select_fusion.5), channel_id=1, source_target_pairs={{0,8},{8,16},{16,24},{1,9},{9,17},{17,25},{2,10},{10,18},{18,26},{... | collective-permute-start | bytes 1572872 | tf_op jit(solution)/shard_map/while/body/eval_jaxpr/ppermute | solution.py:12
Sparse Core Ops, SparseCore 0:
  11.3 28.1 all-gather.2
  47.9 53.5 all-reduce.2
  174.0 31.4 all-gather.4
  214.2 53.5 all-reduce.4
where the time goes:
time: 350 us; the launch traced here: 344 us
  waiting for transfers between devices  249 us (71%)
  matrix products  52 us (15%)
  between operations  13.9 us (4%)
  starting transfers between devices  13.5 us (4%)
  other arithmetic  7.91 us (2%)
  local copies, waits for them, and re-layouts  7.87 us (2%)
    psum x2, waiting for transfers between devices, shards(): station_sum = lax.psum(partial_terms, ('tech', 'blk'))  103 us
    ppermute x9, waiting for transfers between devices, shifted(): return lax.ppermute(block, axis, route)  89.2 us
    all_gather x2, waiting for transfers between devices, shards(): lax.all_gather(residual_low, 'blk', axis=0, tiled=True)  56.5 us
    dot_general x8, matrix products, relay(): jnp.dot(step_matrix, incoming, precision=lax.Precision.HIGHEST)  23.9 us
    ppermute x9, starting transfers between devices, shifted(): return lax.ppermute(block, axis, route)  13.3 us
    dot_general x2, matrix products, shards(): lax.dot_general(coupling_rows, coords.astype(jnp.bfloat16), (((0,), (0,))...  9.82 us
    unnamed x13, local copies, waits for them, and re-layouts  7.54 us
    dot_general x2, matrix products, shards(): jnp.dot(week_inverse, week_rhs + walk_weight[:, None] * later - station_s...  7.18 us
  transfers between devices with their start and end apart: 13, of which 12 were waited for; matrix products, arithmetic and copies ran while one was open for 3% of the time, Pallas kernels for 0%

commit v1 on v0

v1 whole, which is shorter than its diff:
```python
import functools

import jax
import jax.numpy as jnp
from jax import lax
from jax.experimental import pallas as pl
from jax.experimental.pallas import tpu as pltpu
from jax.sharding import PartitionSpec as P

SWEEPS = 2
F32 = jnp.float32
BF16 = jnp.bfloat16
NT = (((1,), (1,)), ((), ()))
TN = (((0,), (0,)), ((), ()))


def split_two(value):
    high = value.astype(BF16)
    return high, (value - high.astype(F32)).astype(BF16)


def kernel(
    weeks,
    groups,
    parts,
    chunk,
    tile,
    inverse_hbm,
    coupling_hbm,
    rhs_hbm,
    seen_ref,
    week_inverse_ref,
    walk_ref,
    week_rhs_ref,
    coords_hbm,
    shared_ref,
    inverse,
    coupling,
    rhs,
    residual,
    arrived,
    coords,
    coords_low,
    seen,
    week_rhs,
    inverse_high,
    inverse_low,
    terms,
    terms_low,
    terms_in,
    shared_low,
    current,
    previous,
    later,
    local_sem,
    gather_send,
    gather_recv,
    terms_send,
    terms_recv,
    shared_send,
    shared_recv,
    chain_send,
    chain_recv,
):
    week = lax.axis_index("chain")
    group = lax.axis_index("tech")
    part = lax.axis_index("blk")
    team = groups * parts
    rank = group * parts + part
    rows = rhs.shape[0]
    piece = current.shape[1]
    chunks = rows // chunk
    not_first = week > 0
    not_last = week < weeks - 1

    def member(number):
        return {"tech": number // parts, "blk": lax.rem(number, parts)}

    def ahead(distance):
        return lax.rem(rank + distance, team)

    def behind(distance):
        return lax.rem(rank + team - distance, team)

    def own_slice(number):
        return pl.ds(pl.multiple_of(number * piece, piece), piece)

    loads = []
    loads.append(pltpu.make_async_copy(rhs_hbm, rhs, local_sem.at[0]))
    for slot in range(parts):
        column = pl.multiple_of(lax.rem(part + parts - slot, parts) * rows, 128)
        loads.append(
            pltpu.make_async_copy(
                inverse_hbm.at[:, pl.ds(column, rows)], inverse.at[slot], local_sem.at[1 + slot]
            )
        )
    loads.append(pltpu.make_async_copy(coupling_hbm, coupling, local_sem.at[1 + parts]))
    for load in loads:
        load.start()

    barrier = pltpu.get_barrier_semaphore()
    for distance in range(1, team):
        pl.semaphore_signal(barrier, inc=1, device_id=member(ahead(distance)))

    @pl.when(not_first)
    def _():
        pl.semaphore_signal(barrier, inc=1, device_id={"chain": week - 1})

    @pl.when(not_last)
    def _():
        pl.semaphore_signal(barrier, inc=1, device_id={"chain": week + 1})

    pl.semaphore_wait(
        barrier, team - 1 + not_first.astype(jnp.int32) + not_last.astype(jnp.int32)
    )

    def gather_copy(sweep, distance, index):
        source = rhs_hbm if sweep == 0 else residual
        span = pl.ds(index * chunk, chunk)
        return pltpu.make_async_remote_copy(
            src_ref=source.at[span],
            dst_ref=arrived.at[sweep, distance - 1, span],
            send_sem=gather_send.at[sweep, distance - 1, index],
            recv_sem=gather_recv.at[sweep, distance - 1, index],
            device_id={"blk": lax.rem(part + distance, parts)},
        )

    def terms_copy(sweep, distance):
        return pltpu.make_async_remote_copy(
            src_ref=terms_low.at[sweep, own_slice(ahead(distance))],
            dst_ref=terms_in.at[sweep, distance - 1],
            send_sem=terms_send.at[sweep, distance - 1],
            recv_sem=terms_recv.at[sweep, distance - 1],
            device_id=member(ahead(distance)),
        )

    def shared_copy(sweep, distance, owner):
        return pltpu.make_async_remote_copy(
            src_ref=shared_low.at[sweep, own_slice(owner)],
            dst_ref=shared_low.at[sweep, own_slice(owner)],
            send_sem=shared_send.at[sweep, distance - 1],
            recv_sem=shared_recv.at[sweep, distance - 1],
            device_id=member(ahead(distance)),
        )

    def onward_copy(sweep):
        return pltpu.make_async_remote_copy(
            src_ref=current.at[sweep],
            dst_ref=previous.at[sweep],
            send_sem=chain_send.at[sweep],
            recv_sem=chain_recv.at[sweep],
            device_id={"chain": lax.rem(week + 1, weeks)},
        )

    def backward_copy(sweep):
        return pltpu.make_async_remote_copy(
            src_ref=current.at[sweep],
            dst_ref=later.at[sweep],
            send_sem=chain_send.at[SWEEPS + sweep],
            recv_sem=chain_recv.at[SWEEPS + sweep],
            device_id={"chain": lax.rem(week + weeks - 1, weeks)},
        )

    def gather_start(sweep, index):
        for distance in range(1, parts):
            gather_copy(sweep, distance, index).start()

    for index in range(chunks):
        gather_start(0, index)

    row_count = seen_ref.shape[1]
    seen[...] = jnp.transpose(jnp.broadcast_to(seen_ref[...], (128, row_count)))
    week_rhs[...] = jnp.transpose(week_rhs_ref[...])
    high, low = split_two(week_inverse_ref[...])
    inverse_high[...] = high
    inverse_low[...] = low
    walk = walk_ref[...]

    def solve_shared(value):
        value_high, value_low = split_two(value)
        first = jnp.dot(
            jnp.concatenate([value_high, value_low], axis=0),
            inverse_high[...],
            preferred_element_type=F32,
        )
        second = jnp.dot(value_high, inverse_low[...], preferred_element_type=F32)
        return first[:piece] + (first[piece:] + second)

    def add_columns(slot, start, width, block, begin):
        @pl.loop(0, rows // tile)
        def _(index):
            span = pl.ds(pl.multiple_of(index * tile, tile), tile)
            product = jnp.dot(
                inverse[slot, span, start : start + width], block, preferred_element_type=F32
            )
            if begin:
                coords[span, :] = product
            else:
                coords[span, :] += product

    for load in loads:
        load.wait()
    coords_out = pltpu.make_async_copy(coords, coords_hbm, local_sem.at[0])
    for sweep in range(SWEEPS):
        if sweep == 0:
            own = rhs
        else:
            own = residual
            for index in range(chunks):
                span = slice(index * chunk, (index + 1) * chunk)
                product = lax.dot_general(
                    coupling[span, :], shared_low[sweep - 1], NT, preferred_element_type=F32
                )
                residual[span, :] = (rhs[span, :].astype(F32) - product).astype(BF16)
                gather_start(sweep, index)
        add_columns(0, 0, rows, own[...], True)
        for index in range(chunks):
            span = slice(index * chunk, (index + 1) * chunk)
            for distance in range(1, parts):
                gather_copy(sweep, distance, index).wait_recv()
                add_columns(
                    distance, index * chunk, chunk, arrived[sweep, distance - 1, span, :], False
                )

        @pl.loop(0, rows // tile)
        def _(index):
            span = pl.ds(pl.multiple_of(index * tile, tile), tile)
            value = coords[span, :] * seen[span, 0:1]
            coords_low[span, :] = value.astype(BF16)
            if sweep == SWEEPS - 1:
                coords[span, :] = value

        if sweep == SWEEPS - 1:
            coords_out.start()
        terms[...] = lax.dot_general(
            coords_low[...], coupling[...], TN, preferred_element_type=F32
        )
        terms_low[sweep] = terms[...].astype(BF16)
        for distance in range(1, team):
            terms_copy(sweep, distance).start()

        right = week_rhs[own_slice(rank), :] - terms[own_slice(rank), :]
        if sweep > 0:
            @pl.when(not_last)
            def _():
                backward_copy(sweep - 1).wait_recv()

            @pl.when(jnp.logical_not(not_last))
            def _():
                later[sweep - 1] = jnp.zeros(later.shape[1:], F32)

            right += walk * later[sweep - 1]
        for distance in range(1, team):
            terms_copy(sweep, distance).wait_recv()
            right -= terms_in[sweep, distance - 1].astype(F32)
        current[sweep] = solve_shared(right)

        @pl.when(not_first)
        def _():
            onward_copy(sweep).wait_recv()
            current[sweep] += solve_shared(walk * previous[sweep])

        @pl.when(not_last)
        def _():
            onward_copy(sweep).start()

        shared_low[sweep, own_slice(rank), :] = current[sweep].astype(BF16)
        for distance in range(1, team):
            shared_copy(sweep, distance, rank).start()
        if sweep < SWEEPS - 1:
            @pl.when(not_first)
            def _():
                backward_copy(sweep).start()

        for distance in range(1, team):
            shared_copy(sweep, distance, behind(distance)).wait_recv()

    shared_ref[...] = shared_low[SWEEPS - 1].astype(F32)

    for sweep in range(SWEEPS):
        for distance in range(1, parts):
            for index in range(chunks):
                gather_copy(sweep, distance, index).wait_send()
        for distance in range(1, team):
            terms_copy(sweep, distance).wait_send()
            shared_copy(sweep, distance, rank).wait_send()

        @pl.when(not_last)
        def _():
            onward_copy(sweep).wait_send()

        if sweep < SWEEPS - 1:
            @pl.when(not_first)
            def _():
                backward_copy(sweep).wait_send()

    coords_out.wait()


def whole_step(size, limit):
    step = min(size, limit)
    while size % step:
        step -= 16
    return step


def shards(
    mesh_shape,
    block_inverse,
    coupling,
    data_rhs,
    station_seen,
    shared_inverse,
    walk_weight,
    shared_rhs,
):
    weeks, groups, parts = (mesh_shape[axis] for axis in ("chain", "tech", "blk"))
    team = groups * parts
    rows, samples = data_rhs.shape[2:]
    width = shared_inverse.shape[1]
    piece = samples // team
    chunk = whole_step(rows, 512)
    tile = whole_step(rows, 512)
    chunks = rows // chunk
    seen_row = jnp.repeat(station_seen[0, 0].astype(F32), 3)[None, :]
    vmem = pl.BlockSpec(memory_space=pltpu.VMEM)
    anywhere = pl.BlockSpec(memory_space=pl.ANY)
    dma = pltpu.SemaphoreType.DMA
    others = max(parts - 1, 1)
    coords, shared = pl.pallas_call(
        functools.partial(kernel, weeks, groups, parts, chunk, tile),
        out_shape=(
            jax.ShapeDtypeStruct((rows, samples), F32),
            jax.ShapeDtypeStruct((samples, width), F32),
        ),
        in_specs=[anywhere] * 3 + [vmem] * 4,
        out_specs=(anywhere, vmem),
        scratch_shapes=[
            pltpu.VMEM((parts, rows, rows), BF16),
            pltpu.VMEM((rows, width), BF16),
            pltpu.VMEM((rows, samples), BF16),
            pltpu.VMEM((rows, samples), BF16),
            pltpu.VMEM((SWEEPS, others, rows, samples), BF16),
            pltpu.VMEM((rows, samples), F32),
            pltpu.VMEM((rows, samples), BF16),
            pltpu.VMEM((rows, 128), F32),
            pltpu.VMEM((samples, width), F32),
            pltpu.VMEM((width, width), BF16),
            pltpu.VMEM((width, width), BF16),
            pltpu.VMEM((samples, width), F32),
            pltpu.VMEM((SWEEPS, samples, width), BF16),
            pltpu.VMEM((SWEEPS, team - 1, piece, width), BF16),
            pltpu.VMEM((SWEEPS, samples, width), BF16),
            pltpu.VMEM((SWEEPS, piece, width), F32),
            pltpu.VMEM((SWEEPS, piece, width), F32),
            pltpu.VMEM((SWEEPS, piece, width), F32),
            dma((2 + parts,)),
            dma((SWEEPS, others, chunks)),
            dma((SWEEPS, others, chunks)),
            dma((SWEEPS, team - 1)),
            dma((SWEEPS, team - 1)),
            dma((SWEEPS, team - 1)),
            dma((SWEEPS, team - 1)),
            dma((2 * SWEEPS,)),
            dma((2 * SWEEPS,)),
        ],
        compiler_params=pltpu.CompilerParams(
            collective_id=0, has_side_effects=True, vmem_limit_bytes=48 * 2**20
        ),
        cost_estimate=pl.CostEstimate(
            flops=2 * SWEEPS * rows * samples * (rows * parts + 2 * width),
            bytes_accessed=2 * rows * (rows * parts + width + samples) + 4 * rows * samples,
            transcendentals=0,
        ),
    )(
        block_inverse[0, 0],
        coupling[0, 0],
        data_rhs[0, 0],
        seen_row,
        shared_inverse[0],
        walk_weight[None, :],
        shared_rhs[0],
    )
    return coords[None, None], shared.T[None]


def solution(mesh):
    in_specs = (
        P("tech", "chain", "blk", None),
        P("tech", "chain", "blk", None),
        P("tech", "chain", "blk", None),
        P("tech", "chain", "blk"),
        P("chain", None, None),
        P(),
        P("chain", None, None),
    )
    out_specs = (P("tech", "chain", "blk", None), P("chain", None, None))
    return jax.shard_map(
        functools.partial(shards, dict(mesh.shape)),
        mesh=mesh,
        in_specs=in_specs,
        out_specs=out_specs,
        check_vma=False,
    )
```

time: 350 us -> 82.9 us (0.24); the launches traced: 344 us -> 82.6 us
  waiting for transfers between devices: 249 us -> 0 us
  Pallas kernels: 0 us -> 73.3 us
  matrix products: 52 us -> 0 us
  starting transfers between devices: 13.5 us -> 0 us
  between operations: 13.9 us -> 0.66 us
  other arithmetic: 7.91 us -> 0.69 us
    psum x2 -> x0, waiting for transfers between devices: 103 us -> none  [shards(): station_sum = lax.psum(partial_terms, ('tech', 'blk'))]
    ppermute x9 -> x0, waiting for transfers between devices: 89.2 us -> none  [shifted(): return lax.ppermute(block, axis, route)]
    pallas_call x0 -> x1, Pallas kernels: none -> 73.3 us  [shards(): pl.pallas_call(functools.partial(kernel, weeks, groups, parts, chunk, til...]
    all_gather x2 -> x0, waiting for transfers between devices: 56.5 us -> none  [shards(): lax.all_gather(residual_low, 'blk', axis=0, tiled=True)]
    dot_general x15 -> x0, matrix products: 52 us -> none  [the longest x8 23.9 us: relay(): jnp.dot(step_matrix, incoming, precision=lax.Precision.HIGHEST)]
    ppermute x9 -> x0, starting transfers between devices: 13.3 us -> none  [shifted(): return lax.ppermute(block, axis, route)]
    while x8 -> x0, other arithmetic: 6.54 us -> none
    unnamed x13 -> x12, local copies, waits for them, and re-layouts: 7.54 us -> 7.62 us
  transfers between devices with their start and end apart: 13 -> 0, of which waited for: 12 -> 0; matrix products, arithmetic and copies ran while one was open for 3% -> 0% of each run, Pallas kernels for 0% -> 0%
where the time goes in v1:
time: 82.9 us; the launch traced here: 82.6 us
  Pallas kernels  73.3 us (88%)
  local copies, waits for them, and re-layouts  7.96 us (10%)
    pallas_call x1, Pallas kernels, shards(): pl.pallas_call(functools.partial(kernel, weeks, groups, parts, chunk, til...  73.3 us
    unnamed x12, local copies, waits for them, and re-layouts  7.62 us

profile of v1, /device:TPU:25, one launch (start us, length us, event | category | flops | bytes accessed | tf_op | source)
XLA Modules:
  0.0 82.6 jit_solution(15114036536009935985)
XLA Ops:
  0.6 0.7 convert_element_type.6
  1.3 0.1 broadcast_in_dim.12
  1.4 0.2 broadcast_in_dim_reshape.3.seen_ref
  1.7 0.0 copy-start
  1.7 1.4 %copy-done = bf16[1,1,1536,512]{3,2,1,0:T(8,128)(2,1)S(1)} copy-done((bf16[1,1,1536,512]{3,2,1,0:T(8,128)(2,1)S(1)}, bf16[1,1,1536,512]{3,2,1,0:T(8,128)(2,1)}, u32[]{:S(2)}) %copy-start) | copy-done | bytes 1572888
  3.1 0.0 copy-start.1
  3.1 1.2 %copy-done.1 = f32[1,512,512]{2,1,0:T(8,128)S(1)} copy-done((f32[1,512,512]{2,1,0:T(8,128)S(1)}, f32[1,512,512]{2,1,0:T(8,128)}, u32[]{:S(2)}) %copy-start.1) | copy-done | bytes 1048600
  4.3 0.0 copy-start.2
  4.3 1.1 %copy-done.2 = bf16[1,1,1536,256]{3,2,1,0:T(8,128)(2,1)S(1)} copy-done((bf16[1,1,1536,256]{3,2,1,0:T(8,128)(2,1)S(1)}, bf16[1,1,1536,256]{3,2,1,0:T(8,128)(2,1)}, u32[]{:S(2)}) %copy-start.2) | copy-done | bytes 786456
  5.4 0.0 copy-start.3
  5.4 1.0 %copy-done.3 = f32[1,512,256]{2,1,0:T(8,128)S(1)} copy-done((f32[1,512,256]{2,1,0:T(8,128)S(1)}, f32[1,512,256]{2,1,0:T(8,128)}, u32[]{:S(2)}) %copy-start.3) | copy-done | bytes 524312
  6.5 0.0 copy-start.4
  6.5 0.7 copy-done.4
  7.2 73.3 %shard_map.86 = (f32[1536,256]{1,0:T(8,128)S(1)}, f32[256,512]{1,0:T(8,128)S(1)}) custom-call(bf16[1536,3072]{1,0:T(8,128)(2,1)} %bitcast.19, bf16[1536,512]{1,0:T(8,128)(2,1)S(1)} %bitcast.13, bf16[1536,256]{1,0:T(8,128)(2,1)S(1)} %bitcast.15, f32[1,1536]{1,0:T(1,128)S(1)} %broadcast_in_dim_reshape.3.seen_ref, f32[512,512]{1,0:T(8,128)S(1)} %bitcast.14, ...), custom_call_target="tpu_custom_call" | custom-call | flops 6442450944 | bytes 13369344 | tf_op jit(solution)/shard_map/pallas_call | solution.py:330
  80.5 1.0 %copy.10 = f32[1,512,256]{2,1,0:T(8,128)} copy(f32[1,512,256]{1,2,0:T(8,128)S(1)} %bitcast.12) | data formatting | bytes 1048576
  81.4 1.1 %copy.12 = f32[1,1,1536,256]{3,2,1,0:T(8,128)} copy(f32[1,1,1536,256]{3,2,1,0:T(8,128)S(1)} %bitcast.11) | data formatting | bytes 3145728
Async XLA Ops:
  1.7 1.4 %copy-start = (bf16[1,1,1536,512]{3,2,1,0:T(8,128)(2,1)S(1)}, bf16[1,1,1536,512]{3,2,1,0:T(8,128)(2,1)}, u32[]{:S(2)}) copy-start(bf16[1,1,1536,512]{3,2,1,0:T(8,128)(2,1)} %param.8) | copy-start | bytes 4718596
  3.1 1.2 %copy-start.1 = (f32[1,512,512]{2,1,0:T(8,128)S(1)}, f32[1,512,512]{2,1,0:T(8,128)}, u32[]{:S(2)}) copy-start(f32[1,512,512]{2,1,0:T(8,128)} %param.11) | copy-start | bytes 3145732
  4.3 1.1 %copy-start.2 = (bf16[1,1,1536,256]{3,2,1,0:T(8,128)(2,1)S(1)}, bf16[1,1,1536,256]{3,2,1,0:T(8,128)(2,1)}, u32[]{:S(2)}) copy-start(bf16[1,1,1536,256]{3,2,1,0:T(8,128)(2,1)} %param.9) | copy-start | bytes 2359300
  5.4 1.0 %copy-start.3 = (f32[1,512,256]{2,1,0:T(8,128)S(1)}, f32[1,512,256]{2,1,0:T(8,128)}, u32[]{:S(2)}) copy-start(f32[1,512,256]{2,1,0:T(8,128)} %param.13) | copy-start | bytes 1572868
  6.5 0.7 copy-start.4

commit v2 on v1

v2 whole, which is shorter than its diff:
```python
import functools

import jax
import jax.numpy as jnp
from jax import lax
from jax.experimental import pallas as pl
from jax.experimental.pallas import tpu as pltpu
from jax.sharding import PartitionSpec as P

SWEEPS = 2
F32 = jnp.float32
BF16 = jnp.bfloat16
NT = (((1,), (1,)), ((), ()))
TN = (((0,), (0,)), ((), ()))


def split_two(value):
    high = value.astype(BF16)
    return high, (value - high.astype(F32)).astype(BF16)


def kernel(
    weeks,
    groups,
    parts,
    halves,
    chunk,
    tile,
    inverse_hbm,
    coupling_hbm,
    rhs_hbm,
    seen_ref,
    week_inverse_hbm,
    walk_ref,
    week_rhs_hbm,
    coords_hbm,
    shared_ref,
    inverse,
    coupling,
    rhs,
    residual,
    arrived,
    coords,
    coords_low,
    seen,
    week_inverse_in,
    week_rhs_in,
    week_rhs,
    inverse_high,
    inverse_low,
    terms,
    terms_low,
    terms_in,
    shared_low,
    current,
    previous,
    later,
    local_sem,
    gather_send,
    gather_recv,
    terms_send,
    terms_recv,
    shared_send,
    shared_recv,
    chain_send,
    chain_recv,
):
    week = lax.axis_index("chain")
    group = lax.axis_index("tech")
    part = lax.axis_index("blk")
    team = groups * parts
    rank = group * parts + part
    rows = rhs.shape[0]
    piece = current.shape[2]
    half_samples = piece * team
    chunks = rows // chunk
    not_first = week > 0
    not_last = week < weeks - 1

    def member(number):
        return {"tech": number // parts, "blk": lax.rem(number, parts)}

    def ahead(distance):
        return lax.rem(rank + distance, team)

    def behind(distance):
        return lax.rem(rank + team - distance, team)

    def own_slice(half, number):
        return pl.ds(pl.multiple_of(half * half_samples + number * piece, piece), piece)

    def half_slice(half):
        return slice(half * half_samples, (half + 1) * half_samples)

    loads = []
    loads.append(pltpu.make_async_copy(rhs_hbm, rhs, local_sem.at[0]))
    for slot in range(parts):
        column = pl.multiple_of(lax.rem(part + parts - slot, parts) * rows, 128)
        loads.append(
            pltpu.make_async_copy(
                inverse_hbm.at[:, pl.ds(column, rows)], inverse.at[slot], local_sem.at[1 + slot]
            )
        )
    loads.append(pltpu.make_async_copy(coupling_hbm, coupling, local_sem.at[1 + parts]))
    loads.append(
        pltpu.make_async_copy(week_inverse_hbm, week_inverse_in, local_sem.at[2 + parts])
    )
    loads.append(pltpu.make_async_copy(week_rhs_hbm, week_rhs_in, local_sem.at[3 + parts]))
    for load in loads:
        load.start()

    barrier = pltpu.get_barrier_semaphore()
    for distance in range(1, team):
        pl.semaphore_signal(barrier, inc=1, device_id=member(ahead(distance)))

    @pl.when(not_first)
    def _():
        pl.semaphore_signal(barrier, inc=1, device_id={"chain": week - 1})

    @pl.when(not_last)
    def _():
        pl.semaphore_signal(barrier, inc=1, device_id={"chain": week + 1})

    pl.semaphore_wait(
        barrier, team - 1 + not_first.astype(jnp.int32) + not_last.astype(jnp.int32)
    )

    def gather_copy(sweep, half, distance, index):
        span = pl.ds(index * chunk, chunk)
        if sweep == 0:
            source = rhs_hbm.at[span, pl.ds(half * half_samples, half_samples)]
        else:
            source = residual.at[half, span]
        return pltpu.make_async_remote_copy(
            src_ref=source,
            dst_ref=arrived.at[sweep, half, distance - 1, span],
            send_sem=gather_send.at[sweep, half, distance - 1, index],
            recv_sem=gather_recv.at[sweep, half, distance - 1, index],
            device_id={"blk": lax.rem(part + distance, parts)},
        )

    def terms_copy(sweep, half, distance):
        return pltpu.make_async_remote_copy(
            src_ref=terms_low.at[sweep, own_slice(half, ahead(distance))],
            dst_ref=terms_in.at[sweep, half, distance - 1],
            send_sem=terms_send.at[sweep, half, distance - 1],
            recv_sem=terms_recv.at[sweep, half, distance - 1],
            device_id=member(ahead(distance)),
        )

    def shared_copy(sweep, half, distance, owner):
        return pltpu.make_async_remote_copy(
            src_ref=shared_low.at[sweep, own_slice(half, owner)],
            dst_ref=shared_low.at[sweep, own_slice(half, owner)],
            send_sem=shared_send.at[sweep, half, distance - 1],
            recv_sem=shared_recv.at[sweep, half, distance - 1],
            device_id=member(ahead(distance)),
        )

    def onward_copy(sweep, half):
        return pltpu.make_async_remote_copy(
            src_ref=current.at[sweep, half],
            dst_ref=previous.at[sweep, half],
            send_sem=chain_send.at[sweep, half],
            recv_sem=chain_recv.at[sweep, half],
            device_id={"chain": lax.rem(week + 1, weeks)},
        )

    def backward_copy(sweep, half):
        return pltpu.make_async_remote_copy(
            src_ref=current.at[sweep, half],
            dst_ref=later.at[sweep, half],
            send_sem=chain_send.at[SWEEPS + sweep, half],
            recv_sem=chain_recv.at[SWEEPS + sweep, half],
            device_id={"chain": lax.rem(week + weeks - 1, weeks)},
        )

    def gather_start(sweep, half, index):
        for distance in range(1, parts):
            gather_copy(sweep, half, distance, index).start()

    for half in range(halves):
        for index in range(chunks):
            gather_start(0, half, index)

    row_count = seen_ref.shape[1]
    seen[...] = jnp.transpose(jnp.broadcast_to(seen_ref[...], (128, row_count)))
    for load in loads:
        load.wait()
    week_rhs[...] = jnp.transpose(week_rhs_in[...])
    high, low = split_two(week_inverse_in[...])
    inverse_high[...] = high
    inverse_low[...] = low
    walk = walk_ref[...]

    def solve_shared(value):
        value_high, value_low = split_two(value)
        first = jnp.dot(
            jnp.concatenate([value_high, value_low], axis=0),
            inverse_high[...],
            preferred_element_type=F32,
        )
        second = jnp.dot(value_high, inverse_low[...], preferred_element_type=F32)
        return first[:piece] + (first[piece:] + second)

    def add_columns(half, slot, start, width, block, begin):
        @pl.loop(0, rows // tile)
        def _(index):
            span = pl.ds(pl.multiple_of(index * tile, tile), tile)
            product = jnp.dot(
                inverse[slot, span, start : start + width], block, preferred_element_type=F32
            )
            if begin:
                coords[span, half_slice(half)] = product
            else:
                coords[span, half_slice(half)] += product

    def make_residual(sweep, half):
        for distance in range(1, team):
            shared_copy(sweep - 1, half, distance, behind(distance)).wait_recv()
        for index in range(chunks):
            span = slice(index * chunk, (index + 1) * chunk)
            product = lax.dot_general(
                coupling[span, :],
                shared_low[sweep - 1, half_slice(half), :],
                NT,
                preferred_element_type=F32,
            )
            residual[half, span, :] = (
                rhs[span, half_slice(half)].astype(F32) - product
            ).astype(BF16)
            gather_start(sweep, half, index)

    def make_terms(sweep, half):
        own = rhs[:, half_slice(half)] if sweep == 0 else residual[half]
        add_columns(half, 0, 0, rows, own, True)
        for index in range(chunks):
            span = slice(index * chunk, (index + 1) * chunk)
            for distance in range(1, parts):
                gather_copy(sweep, half, distance, index).wait_recv()
                block = arrived[sweep, half, distance - 1, span, :]
                add_columns(half, distance, index * chunk, chunk, block, False)

        @pl.loop(0, rows // tile)
        def _(index):
            span = pl.ds(pl.multiple_of(index * tile, tile), tile)
            value = coords[span, half_slice(half)] * seen[span, 0:1]
            coords_low[span, :] = value.astype(BF16)
            if sweep == SWEEPS - 1:
                coords[span, half_slice(half)] = value

        product = lax.dot_general(
            coords_low[...], coupling[...], TN, preferred_element_type=F32
        )
        terms[half_slice(half), :] = product
        terms_low[sweep, half_slice(half), :] = product.astype(BF16)
        for distance in range(1, team):
            terms_copy(sweep, half, distance).start()

    def make_shared(sweep, half):
        own = own_slice(half, rank)
        right = week_rhs[own, :] - terms[own, :]
        if sweep > 0:
            @pl.when(not_last)
            def _():
                backward_copy(sweep - 1, half).wait_recv()

            @pl.when(jnp.logical_not(not_last))
            def _():
                later[sweep - 1, half] = jnp.zeros(later.shape[2:], F32)

            right += walk * later[sweep - 1, half]
        for distance in range(1, team):
            terms_copy(sweep, half, distance).wait_recv()
            right -= terms_in[sweep, half, distance - 1].astype(F32)
        current[sweep, half] = solve_shared(right)

        @pl.when(not_first)
        def _():
            onward_copy(sweep, half).wait_recv()
            current[sweep, half] += solve_shared(walk * previous[sweep, half])

        @pl.when(not_last)
        def _():
            onward_copy(sweep, half).start()

        shared_low[sweep, own, :] = current[sweep, half].astype(BF16)
        for distance in range(1, team):
            shared_copy(sweep, half, distance, rank).start()
        if sweep < SWEEPS - 1:
            @pl.when(not_first)
            def _():
                backward_copy(sweep, half).start()

    coords_out = pltpu.make_async_copy(coords, coords_hbm, local_sem.at[0])

    for sweep in range(SWEEPS):
        for half in range(halves):
            make_terms(sweep, half)
            if sweep == SWEEPS - 1 and half == halves - 1:
                coords_out.start()
            if sweep < SWEEPS - 1 and half > 0:
                make_residual(sweep + 1, half - 1)
            make_shared(sweep, half)
        if sweep < SWEEPS - 1:
            make_residual(sweep + 1, halves - 1)
        else:
            for half in range(halves):
                for distance in range(1, team):
                    shared_copy(sweep, half, distance, behind(distance)).wait_recv()

    shared_ref[...] = shared_low[SWEEPS - 1].astype(F32)

    for sweep in range(SWEEPS):
        for half in range(halves):
            for distance in range(1, parts):
                for index in range(chunks):
                    gather_copy(sweep, half, distance, index).wait_send()
            for distance in range(1, team):
                terms_copy(sweep, half, distance).wait_send()
                shared_copy(sweep, half, distance, rank).wait_send()

            @pl.when(not_last)
            def _():
                onward_copy(sweep, half).wait_send()

            if sweep < SWEEPS - 1:
                @pl.when(not_first)
                def _():
                    backward_copy(sweep, half).wait_send()

    coords_out.wait()


def whole_step(size, limit):
    step = min(size, limit)
    while size % step:
        step -= 16
    return step


def shards(
    mesh_shape,
    block_inverse,
    coupling,
    data_rhs,
    station_seen,
    shared_inverse,
    walk_weight,
    shared_rhs,
):
    weeks, groups, parts = (mesh_shape[axis] for axis in ("chain", "tech", "blk"))
    team = groups * parts
    rows, samples = data_rhs.shape[2:]
    width = shared_inverse.shape[1]
    halves = 2 if samples % (2 * max(128, 16 * team)) == 0 else 1
    half_samples = samples // halves
    piece = half_samples // team
    chunk = whole_step(rows, 512)
    tile = whole_step(rows, 512)
    chunks = rows // chunk
    seen_row = jnp.repeat(station_seen[0, 0].astype(F32), 3)[None, :]
    vmem = pl.BlockSpec(memory_space=pltpu.VMEM)
    anywhere = pl.BlockSpec(memory_space=pl.ANY)
    dma = pltpu.SemaphoreType.DMA
    others = max(parts - 1, 1)
    coords, shared = pl.pallas_call(
        functools.partial(kernel, weeks, groups, parts, halves, chunk, tile),
        out_shape=(
            jax.ShapeDtypeStruct((rows, samples), F32),
            jax.ShapeDtypeStruct((samples, width), F32),
        ),
        in_specs=[anywhere] * 3 + [vmem, anywhere, vmem, anywhere],
        out_specs=(anywhere, vmem),
        scratch_shapes=[
            pltpu.VMEM((parts, rows, rows), BF16),
            pltpu.VMEM((rows, width), BF16),
            pltpu.VMEM((rows, samples), BF16),
            pltpu.VMEM((halves, rows, half_samples), BF16),
            pltpu.VMEM((SWEEPS, halves, others, rows, half_samples), BF16),
            pltpu.VMEM((rows, samples), F32),
            pltpu.VMEM((rows, half_samples), BF16),
            pltpu.VMEM((rows, 128), F32),
            pltpu.VMEM((width, width), F32),
            pltpu.VMEM((width, samples), F32),
            pltpu.VMEM((samples, width), F32),
            pltpu.VMEM((width, width), BF16),
            pltpu.VMEM((width, width), BF16),
            pltpu.VMEM((samples, width), F32),
            pltpu.VMEM((SWEEPS, samples, width), BF16),
            pltpu.VMEM((SWEEPS, halves, team - 1, piece, width), BF16),
            pltpu.VMEM((SWEEPS, samples, width), BF16),
            pltpu.VMEM((SWEEPS, halves, piece, width), F32),
            pltpu.VMEM((SWEEPS, halves, piece, width), F32),
            pltpu.VMEM((SWEEPS, halves, piece, width), F32),
            dma((4 + parts,)),
            dma((SWEEPS, halves, others, chunks)),
            dma((SWEEPS, halves, others, chunks)),
            dma((SWEEPS, halves, team - 1)),
            dma((SWEEPS, halves, team - 1)),
            dma((SWEEPS, halves, team - 1)),
            dma((SWEEPS, halves, team - 1)),
            dma((2 * SWEEPS, halves)),
            dma((2 * SWEEPS, halves)),
        ],
        compiler_params=pltpu.CompilerParams(
            collective_id=0, has_side_effects=True, vmem_limit_bytes=60 * 2**20
        ),
        cost_estimate=pl.CostEstimate(
            flops=2 * SWEEPS * rows * samples * (rows * parts + 2 * width),
            bytes_accessed=2 * rows * (rows * parts + width + samples) + 4 * rows * samples,
            transcendentals=0,
        ),
    )(
        block_inverse[0, 0],
        coupling[0, 0],
        data_rhs[0, 0],
        seen_row,
        shared_inverse[0],
        walk_weight[None, :],
        shared_rhs[0],
    )
    return coords[None, None], shared.T[None]


def solution(mesh):
    in_specs = (
        P("tech", "chain", "blk", None),
        P("tech", "chain", "blk", None),
        P("tech", "chain", "blk", None),
        P("tech", "chain", "blk"),
        P("chain", None, None),
        P(),
        P("chain", None, None),
    )
    out_specs = (P("tech", "chain", "blk", None), P("chain", None, None))
    return jax.shard_map(
        functools.partial(shards, dict(mesh.shape)),
        mesh=mesh,
        in_specs=in_specs,
        out_specs=out_specs,
        check_vma=False,
    )
```

time: 82.9 us -> 84.2 us (1.016)
  Pallas kernels: 73.3 us -> 77 us
  local copies, waits for them, and re-layouts: 7.96 us -> 5.63 us
    pallas_call x1, Pallas kernels: 73.3 us -> 77 us  [shards(): pl.pallas_call(functools.partial(kernel, weeks, groups, parts, halves, ch...]
    unnamed x12 -> x2, local copies, waits for them, and re-layouts: 7.62 us -> 4.69 us
where the time goes in v2:
time: 84.2 us; the launch traced here: 84 us
  Pallas kernels  77 us (91%)
  local copies, waits for them, and re-layouts  5.63 us (7%)
    pallas_call x1, Pallas kernels, shards(): pl.pallas_call(functools.partial(kernel, weeks, groups, parts, halves, ch...  77 us
    unnamed x2, local copies, waits for them, and re-layouts  4.69 us

profile of v2, /device:TPU:25, one launch (start us, length us, event | category | flops | bytes accessed | tf_op | source)
XLA Modules:
  0.0 84.0 jit_solution(4695357063468114559)
XLA Ops:
  0.6 0.7 convert_element_type.6
  1.3 0.1 broadcast_in_dim.12
  1.4 0.8 broadcast_in_dim_reshape.3.seen_ref
  2.3 77.0 %shard_map.86 = (f32[1536,256]{1,0:T(8,128)}, f32[256,512]{1,0:T(8,128)}) custom-call(bf16[1536,3072]{1,0:T(8,128)(2,1)} %bitcast.14, bf16[1536,512]{1,0:T(8,128)(2,1)} %bitcast.15, bf16[1536,256]{1,0:T(8,128)(2,1)} %bitcast.17, f32[1,1536]{1,0:T(1,128)} %broadcast_in_dim_reshape.3.seen_ref, f32[512,512]{1,0:T(8,128)} %bitcast.16, f32[1,512]{1,0:T(1,128)} %bitcast.19, ...), custom_call_target="tpu_custom_call" | custom-call | flops 6442450944 | bytes 13369344 | tf_op jit(solution)/shard_map/pallas_call | solution.py:367
  79.3 2.0 %copy.10 = f32[1,512,256]{2,1,0:T(8,128)} copy(f32[1,512,256]{1,2,0:T(8,128)} %bitcast.12) | data formatting | bytes 1048576
  81.3 2.7 %copy.12 = f32[1,1,1536,256]{3,2,1,0:T(8,128)} copy(f32[1,1,1536,256]{3,2,1,0:T(8,128)} %bitcast.11) | data formatting | bytes 3145728

commit v3 on v2

--- a/solution.py
+++ b/solution.py
@@ -8,6 +8,7 @@
 from jax.sharding import PartitionSpec as P
 
 SWEEPS = 2
+HALVES = 1
 F32 = jnp.float32
 BF16 = jnp.bfloat16
 NT = (((1,), (1,)), ((), ()))
@@ -183,8 +184,19 @@
         for index in range(chunks):
             gather_start(0, half, index)
 
-    row_count = seen_ref.shape[1]
-    seen[...] = jnp.transpose(jnp.broadcast_to(seen_ref[...], (128, row_count)))
+    stations = seen_ref.shape[1]
+    per_station = rows // stations
+
+    @pl.loop(0, rows // tile)
+    def _(index):
+        start = pl.multiple_of(index * tile, tile)
+        row = start + lax.broadcasted_iota(jnp.int32, (tile, stations), 0)
+        offset = row - per_station * lax.broadcasted_iota(jnp.int32, (tile, stations), 1)
+        inside = jnp.logical_and(offset >= 0, offset < per_station)
+        picked = jnp.where(inside, seen_ref[...].astype(F32), 0.0)
+        column = jnp.sum(picked, axis=1, keepdims=True)
+        seen[pl.ds(start, tile), :] = jnp.broadcast_to(column, (tile, 128))
+
     for load in loads:
         load.wait()
     week_rhs[...] = jnp.transpose(week_rhs_in[...])
@@ -353,13 +365,12 @@
     team = groups * parts
     rows, samples = data_rhs.shape[2:]
     width = shared_inverse.shape[1]
-    halves = 2 if samples % (2 * max(128, 16 * team)) == 0 else 1
+    halves = HALVES
     half_samples = samples // halves
     piece = half_samples // team
     chunk = whole_step(rows, 512)
     tile = whole_step(rows, 512)
     chunks = rows // chunk
-    seen_row = jnp.repeat(station_seen[0, 0].astype(F32), 3)[None, :]
     vmem = pl.BlockSpec(memory_space=pltpu.VMEM)
     anywhere = pl.BlockSpec(memory_space=pl.ANY)
     dma = pltpu.SemaphoreType.DMA
@@ -415,7 +426,7 @@
         block_inverse[0, 0],
         coupling[0, 0],
         data_rhs[0, 0],
-        seen_row,
+        station_seen[0],
         shared_inverse[0],
         walk_weight[None, :],
         shared_rhs[0],

time: 84.2 us -> 80.2 us (0.952)
  Pallas kernels: 77 us -> 74.7 us
  local copies, waits for them, and re-layouts: 5.63 us -> 4.69 us
    pallas_call x1, Pallas kernels: 77 us -> 74.7 us  [shards(): pl.pallas_call(functools.partial(kernel, weeks, groups, parts, halves, ch...]
where the time goes in v3:
time: 80.2 us; the launch traced here: 80 us
  Pallas kernels  74.7 us (93%)
  local copies, waits for them, and re-layouts  4.69 us (6%)
    pallas_call x1, Pallas kernels, shards(): pl.pallas_call(functools.partial(kernel, weeks, groups, parts, halves, ch...  74.7 us
    unnamed x2, local copies, waits for them, and re-layouts  4.69 us

profile of v3, /device:TPU:25, one launch (start us, length us, event | category | flops | bytes accessed | tf_op | source)
XLA Modules:
  0.0 80.0 jit_solution(8733548669258261170)
XLA Ops:
  0.6 74.7 %shard_map.86 = (f32[1536,256]{1,0:T(8,128)}, f32[256,512]{1,0:T(8,128)}) custom-call(bf16[1536,3072]{1,0:T(8,128)(2,1)} %bitcast.13, bf16[1536,512]{1,0:T(8,128)(2,1)} %bitcast.14, bf16[1536,256]{1,0:T(8,128)(2,1)} %bitcast.16, s32[1,512]{1,0:T(1,128)} %bitcast.18, f32[512,512]{1,0:T(8,128)} %bitcast.15, f32[1,512]{1,0:T(1,128)} %bitcast.19, ...), custom_call_target="tpu_custom_call" | custom-call | flops 6442450944 | bytes 13369344 | tf_op jit(solution)/shard_map/pallas_call | solution.py:378
  75.3 2.0 %copy.9 = f32[1,512,256]{2,1,0:T(8,128)} copy(f32[1,512,256]{1,2,0:T(8,128)} %bitcast.12) | data formatting | bytes 1048576
  77.4 2.7 %copy.11 = f32[1,1,1536,256]{3,2,1,0:T(8,128)} copy(f32[1,1,1536,256]{3,2,1,0:T(8,128)} %bitcast.11) | data formatting | bytes 3145728

commit v4 on v3

--- a/solution.py
+++ b/solution.py
@@ -41,6 +41,7 @@
     rhs,
     residual,
     arrived,
+    coupling_in,
     coords,
     coords_low,
     seen,
@@ -65,6 +66,8 @@
     shared_recv,
     chain_send,
     chain_recv,
+    early_send,
+    early_recv,
 ):
     week = lax.axis_index("chain")
     group = lax.axis_index("tech")
@@ -137,6 +140,17 @@
             dst_ref=arrived.at[sweep, half, distance - 1, span],
             send_sem=gather_send.at[sweep, half, distance - 1, index],
             recv_sem=gather_recv.at[sweep, half, distance - 1, index],
+            device_id={"blk": lax.rem(part + distance, parts)},
+        )
+
+    last = pl.ds((chunks - 1) * chunk, chunk)
+
+    def early_copy(distance):
+        return pltpu.make_async_remote_copy(
+            src_ref=coupling.at[last],
+            dst_ref=coupling_in.at[distance - 1],
+            send_sem=early_send.at[distance - 1],
+            recv_sem=early_recv.at[distance - 1],
             device_id={"blk": lax.rem(part + distance, parts)},
         )
 
@@ -241,16 +255,32 @@
             residual[half, span, :] = (
                 rhs[span, half_slice(half)].astype(F32) - product
             ).astype(BF16)
-            gather_start(sweep, half, index)
+            if index < chunks - 1:
+                gather_start(sweep, half, index)
 
     def make_terms(sweep, half):
         own = rhs[:, half_slice(half)] if sweep == 0 else residual[half]
         add_columns(half, 0, 0, rows, own, True)
-        for index in range(chunks):
+        if sweep > 0:
+            for distance in range(1, parts):
+                if sweep == 1 and half == 0:
+                    early_copy(distance).wait_recv()
+                product = lax.dot_general(
+                    coupling_in[distance - 1],
+                    shared_low[sweep - 1, half_slice(half), :],
+                    NT,
+                    preferred_element_type=F32,
+                )
+                first = arrived[0, half, distance - 1, last, :].astype(F32)
+                block = (first - product).astype(BF16)
+                add_columns(half, distance, (chunks - 1) * chunk, chunk, block, False)
+        for index in range(chunks if sweep == 0 else chunks - 1):
             span = slice(index * chunk, (index + 1) * chunk)
             for distance in range(1, parts):
                 gather_copy(sweep, half, distance, index).wait_recv()
                 block = arrived[sweep, half, distance - 1, span, :]
+                if sweep == 0 and half == halves - 1 and index == chunks - 1:
+                    early_copy(distance).start()
                 add_columns(half, distance, index * chunk, chunk, block, False)
 
         @pl.loop(0, rows // tile)
@@ -326,7 +356,7 @@
     for sweep in range(SWEEPS):
         for half in range(halves):
             for distance in range(1, parts):
-                for index in range(chunks):
+                for index in range(chunks if sweep == 0 else chunks - 1):
                     gather_copy(sweep, half, distance, index).wait_send()
             for distance in range(1, team):
                 terms_copy(sweep, half, distance).wait_send()
@@ -341,6 +371,8 @@
                 def _():
                     backward_copy(sweep, half).wait_send()
 
+    for distance in range(1, parts):
+        early_copy(distance).wait_send()
     coords_out.wait()
 
 
@@ -389,6 +421,7 @@
             pltpu.VMEM((rows, samples), BF16),
             pltpu.VMEM((halves, rows, half_samples), BF16),
             pltpu.VMEM((SWEEPS, halves, others, rows, half_samples), BF16),
+            pltpu.VMEM((others, chunk, width), BF16),
             pltpu.VMEM((rows, samples), F32),
             pltpu.VMEM((rows, half_samples), BF16),
             pltpu.VMEM((rows, 128), F32),
@@ -413,6 +446,8 @@
             dma((SWEEPS, halves, team - 1)),
             dma((2 * SWEEPS, halves)),
             dma((2 * SWEEPS, halves)),
+            dma((others,)),
+            dma((others,)),
         ],
         compiler_params=pltpu.CompilerParams(
             collective_id=0, has_side_effects=True, vmem_limit_bytes=60 * 2**20

time: 80.2 us -> 83.9 us (1.046)
  Pallas kernels: 74.7 us -> 78.1 us
    pallas_call x1, Pallas kernels: 74.7 us -> 78.1 us  [shards(): pl.pallas_call(functools.partial(kernel, weeks, groups, parts, halves, ch...]
where the time goes in v4:
time: 83.9 us; the launch traced here: 83.5 us
  Pallas kernels  78.1 us (93%)
  local copies, waits for them, and re-layouts  4.69 us (6%)
    pallas_call x1, Pallas kernels, shards(): pl.pallas_call(functools.partial(kernel, weeks, groups, parts, halves, ch...  78.1 us
    unnamed x2, local copies, waits for them, and re-layouts  4.69 us

profile of v4, /device:TPU:25, one launch (start us, length us, event | category | flops | bytes accessed | tf_op | source)
XLA Modules:
  0.0 83.5 jit_solution(6908273913118212581)
XLA Ops:
  0.6 78.1 %shard_map.86 = (f32[1536,256]{1,0:T(8,128)}, f32[256,512]{1,0:T(8,128)}) custom-call(bf16[1536,3072]{1,0:T(8,128)(2,1)} %bitcast.13, bf16[1536,512]{1,0:T(8,128)(2,1)} %bitcast.14, bf16[1536,256]{1,0:T(8,128)(2,1)} %bitcast.16, s32[1,512]{1,0:T(1,128)} %bitcast.18, f32[512,512]{1,0:T(8,128)} %bitcast.15, f32[1,512]{1,0:T(1,128)} %bitcast.19, ...), custom_call_target="tpu_custom_call" | custom-call | flops 6442450944 | bytes 13369344 | tf_op jit(solution)/shard_map/pallas_call | solution.py:410
  78.8 2.0 %copy.9 = f32[1,512,256]{2,1,0:T(8,128)} copy(f32[1,512,256]{1,2,0:T(8,128)} %bitcast.12) | data formatting | bytes 1048576
  80.8 2.7 %copy.11 = f32[1,1,1536,256]{3,2,1,0:T(8,128)} copy(f32[1,1,1536,256]{3,2,1,0:T(8,128)} %bitcast.11) | data formatting | bytes 3145728
